TPU v7x, 512 devices: a whole 4x4x16 slice. The times are simulated.
512 devices in a mesh: space: 8 (over y, core), energy: 64 (over x, z).
Axes of the slice: x: 4, y: 4, z: 16, core: 2. Of those that a mesh axis runs over, the one named last changes fastest.
Arguments:
- green_lesser: bfloat16 [64, 8, 2, 256, 256], P('energy', 'space'), may hold values from -6 to 6
- screened_lesser: bfloat16 [64, 8, 2, 256, 256], P('energy', 'space'), may hold values from -0.75 to 0.75
- green_retarded: bfloat16 [64, 8, 2, 256, 256], P('energy', 'space'), may hold values from -6 to 6
- screened_retarded: bfloat16 [64, 8, 2, 256, 256], P('energy', 'space'), may hold values from -0.75 to 0.75
- left_green: bfloat16 [64, 8, 2, 256, 256], P('energy', 'space'), may hold values from -0.25 to 0.25
- coupling: bfloat16 [8, 2, 256, 256], P('space'), may hold values from -0.25 to 0.25
Outputs:
- lesser_left: bfloat16 [64, 8, 2, 256, 256], P('energy', 'space')
- sigma_retarded: bfloat16 [64, 8, 2, 256, 256], P('energy', 'space')
All inputs are finite; a program needn't handle non-finite values.
Results may differ from a plain program's by a relative error of at most 0.018.
Values may be sent and summed in bfloat16 or wider, within the bound.
A program may use at most 64 MiB of HBM per device.

v0:
```python
import math

import jax
import jax.numpy as jnp
from jax import lax
from jax.sharding import PartitionSpec as P


def from_behind(array, axis, by):
    size = lax.axis_size(axis)
    pairs = [(i, i + by) for i in range(size) if 0 <= i + by < size]
    return lax.ppermute(array, axis, pairs)


def contract(einsum_pattern, first_factor, second_factor):
    return jnp.einsum(
        einsum_pattern,
        first_factor,
        second_factor,
        precision=lax.Precision.HIGHEST,
        preferred_element_type=jnp.float32,
    )


def complex_product(einsum_pattern, first_factor, second_factor):
    first_real, first_imag = (first_factor[..., 0, :, :], first_factor[..., 1, :, :])
    second_real, second_imag = (second_factor[..., 0, :, :], second_factor[..., 1, :, :])
    real_part = contract(einsum_pattern, first_real, second_real) - contract(
        einsum_pattern, first_imag, second_imag
    )
    imag_part = contract(einsum_pattern, first_real, second_imag) + contract(
        einsum_pattern, first_imag, second_real
    )
    return jnp.stack([real_part, imag_part], axis=-3)


def adjoint_product(einsum_pattern, first_factor, second_factor):
    first_real, first_imag = (first_factor[..., 0, :, :], first_factor[..., 1, :, :])
    second_real, second_imag = (second_factor[..., 0, :, :], second_factor[..., 1, :, :])
    real_part = contract(einsum_pattern, first_real, second_real) + contract(
        einsum_pattern, first_imag, second_imag
    )
    imag_part = contract(einsum_pattern, first_imag, second_real) - contract(
        einsum_pattern, first_real, second_imag
    )
    return jnp.stack([real_part, imag_part], axis=-3)


def rounded(values):
    return lax.optimization_barrier(values.astype(jnp.bfloat16))


def sandwich(propagator, state):
    inner = complex_product("eij,ejk->eik", propagator, state)
    return adjoint_product("eij,ekj->eik", inner, propagator)


def split_parts(values):
    upper_block = values.astype(jnp.bfloat16)
    lower = (values - upper_block.astype(jnp.float32)).astype(jnp.bfloat16)
    return (upper_block, lower)


def trig_table(phase, length):
    angle = phase.astype(jnp.float32) * (2.0 * math.pi / length)
    return (split_parts(jnp.cos(angle)), split_parts(jnp.sin(angle)))


def table_product(trig_table_pair, slab_values):
    upper_block = jnp.einsum(
        "jz,zgx->jgx", trig_table_pair[0], slab_values, preferred_element_type=jnp.float32
    )
    return upper_block + jnp.einsum(
        "jz,zgx->jgx", trig_table_pair[1], slab_values, preferred_element_type=jnp.float32
    )


def table_product_wide(trig_table_pair, slab_values):
    upper_values, lower_values = split_parts(slab_values)
    total_sum = jnp.einsum(
        "jz,zgx->jgx", trig_table_pair[0], upper_values, preferred_element_type=jnp.float32
    )
    total_sum = total_sum + jnp.einsum(
        "jz,zgx->jgx", trig_table_pair[0], lower_values, preferred_element_type=jnp.float32
    )
    return total_sum + jnp.einsum(
        "jz,zgx->jgx", trig_table_pair[1], upper_values, preferred_element_type=jnp.float32
    )


def transform(table, real_part, imag_part, backward):
    cosine_table, sine_table = table
    if backward:
        cos_real = table_product_wide(cosine_table, real_part)
        cos_imag = table_product_wide(cosine_table, imag_part)
        sin_real = table_product_wide(sine_table, real_part)
        sin_imag = table_product_wide(sine_table, imag_part)
        return (cos_real - sin_imag, cos_imag + sin_real)
    cos_real = table_product(cosine_table, real_part)
    cos_imag = table_product(cosine_table, imag_part)
    sin_real = table_product(sine_table, real_part)
    sin_imag = table_product(sine_table, imag_part)
    return (cos_real + sin_imag, cos_imag - sin_real)


def pair_product(first_pair, second_pair):
    return (
        first_pair[0] * second_pair[0] - first_pair[1] * second_pair[1],
        first_pair[0] * second_pair[1] + first_pair[1] * second_pair[0],
    )


def convolve(pieces):
    piece_shape = pieces[0].shape
    energies_all = piece_shape[0]
    length = 2 * energies_all
    freq_index = jnp.arange(length, dtype=jnp.int32)
    energy_index = jnp.arange(energies_all, dtype=jnp.int32)
    lag_index = energy_index - energies_all // 2
    green_table = trig_table(freq_index[:, None] * energy_index[None, :] % length, length)
    screen_table = trig_table(freq_index[:, None] * lag_index[None, :] % length, length)
    return_table = trig_table(energy_index[:, None] * freq_index[None, :] % length, length)

    def spectrum(stacked, table):
        flat = stacked.reshape(piece_shape[0], piece_shape[1], 2, piece_shape[3] * piece_shape[4])
        return transform(table, flat[:, :, 0], flat[:, :, 1], False)

    green_less = spectrum(pieces[0], green_table)
    screen_less = spectrum(pieces[1], screen_table)
    green_ret = spectrum(pieces[2], green_table)
    screen_ret = spectrum(pieces[3], screen_table)
    lesser_hat = pair_product(green_less, screen_less)
    screen_total = (screen_less[0] + screen_ret[0], screen_less[1] + screen_ret[1])
    first_term = pair_product(green_ret, screen_total)
    second_term = pair_product(green_less, screen_ret)
    retarded_hat = (first_term[0] + second_term[0], first_term[1] + second_term[1])

    def to_energy(spectrum_pair):
        real_part, imag_part = transform(return_table, spectrum_pair[0], spectrum_pair[1], True)
        stacked = jnp.stack([real_part, imag_part], axis=2) * (1.0 / length)
        return stacked.reshape(piece_shape).astype(jnp.bfloat16)

    lesser_sigma = to_energy(lesser_hat)
    retarded_sigma = to_energy(retarded_hat)
    return (
        lax.all_to_all(lesser_sigma, "energy", split_axis=0, concat_axis=3, tiled=True),
        lax.all_to_all(retarded_sigma, "energy", split_axis=0, concat_axis=3, tiled=True),
    )


def body(green_lesser, screened_lesser, green_retarded, screened_retarded, left_green, coupling):
    energy_points, slabs, _, order, _ = green_lesser.shape
    sigma_lesser, sigma_retarded = convolve(
        (
            lax.all_to_all(green_lesser, "energy", split_axis=3, concat_axis=0, tiled=True),
            lax.all_to_all(screened_lesser, "energy", split_axis=3, concat_axis=0, tiled=True),
            lax.all_to_all(green_retarded, "energy", split_axis=3, concat_axis=0, tiled=True),
            lax.all_to_all(screened_retarded, "energy", split_axis=3, concat_axis=0, tiled=True),
        )
    )
    propagator = rounded(complex_product("esij,sjk->esik", left_green, coupling)).astype(
        jnp.float32
    )
    half_source = rounded(complex_product("esij,esjk->esik", left_green, sigma_lesser))
    source = adjoint_product("esij,eskj->esik", half_source, left_green)
    slab_props = jnp.swapaxes(propagator, 0, 1)
    slab_sources = jnp.swapaxes(source, 0, 1)

    def final_state(entering):

        def state_step(state, slab_pair):
            return (slab_pair[1] + sandwich(slab_pair[0], state), None)

        return lax.scan(state_step, entering, (slab_props, slab_sources))[0]

    zero_state = jnp.zeros((energy_points, 2, order, order), jnp.float32)
    position = lax.axis_index("space")
    devices = lax.axis_size("space")

    def relay_turn(turn_index, entering):
        leaving = lax.cond(position == turn_index, final_state, jnp.zeros_like, entering)
        received = from_behind(leaving.astype(jnp.bfloat16), "space", 1).astype(leaving.dtype)
        return jnp.where(position == turn_index + 1, received, entering)

    entering = lax.fori_loop(0, devices - 1, relay_turn, zero_state)

    def slab_step(state, slab_pair):
        new_state = slab_pair[1] + sandwich(slab_pair[0], state)
        return (new_state, new_state.astype(jnp.bfloat16))

    _, outputs = lax.scan(slab_step, entering, (slab_props, slab_sources))
    lesser_left = jnp.swapaxes(outputs, 0, 1)
    return (lesser_left, sigma_retarded)


def solution(mesh):
    in_specs = (
        P("energy", "space", None, None, None),
        P("energy", "space", None, None, None),
        P("energy", "space", None, None, None),
        P("energy", "space", None, None, None),
        P("energy", "space", None, None, None),
        P("space", None, None, None),
    )
    out_specs = (P("energy", "space", None, None, None), P("energy", "space", None, None, None))
    return jax.shard_map(body, mesh=mesh, in_specs=in_specs, out_specs=out_specs, check_vma=False)
```

profile of v0, /device:TPU:24, one launch (start us, length us, event | category | flops | bytes accessed | tf_op | source)
XLA Modules:
  0.0 258.5 jit_solution(7154432147454395261)
XLA Ops:
  0.6 1.9 copy.34
  2.6 18.7 %all-to-all-start = ((bf16[1,1,2,256,256]{4,2,1,0,3:T(2,128)(2,1)}), bf16[1,1,2,256,256]{4,2,1,0,3:T(2,128)(2,1)S(1)}, u32[]{:S(2)}, u32[]{:S(2)}) async-start(bf16[1,1,2,256,256]{4,2,1,0,3:T(2,128)(2,1)} %copy.34), calls=%async_computation | async-start | bytes 524288 | tf_op jit(solution)/shard_map/all_to_all | solution.py:155
  22.2 20.0 %all-to-all-done = bf16[1,1,2,256,256]{4,2,1,0,3:T(2,128)(2,1)S(1)} async-done(((bf16[1,1,2,256,256]{4,2,1,0,3:T(2,128)(2,1)}), bf16[1,1,2,256,256]{4,2,1,0,3:T(2,128)(2,1)S(1)}, u32[]{:S(2)}, u32[]{:S(2)}) %all-to-all-start) | async-done | bytes 262176 | tf_op jit(solution)/shard_map/all_to_all | solution.py:155
  42.2 6.5 %all-to-all-start.1 = ((bf16[1,1,2,256,256]{4,2,1,0,3:T(2,128)(2,1)}), bf16[1,1,2,256,256]{4,2,1,0,3:T(2,128)(2,1)S(1)}, u32[]{:S(2)}, u32[]{:S(2)}) async-start(bf16[1,1,2,256,256]{4,2,1,0,3:T(2,128)(2,1)} %copy.36), calls=%async_computation.1 | async-start | bytes 524288 | tf_op jit(solution)/shard_map/all_to_all | solution.py:156
  52.1 16.8 %all-to-all-done.1 = bf16[1,1,2,256,256]{4,2,1,0,3:T(2,128)(2,1)S(1)} async-done(((bf16[1,1,2,256,256]{4,2,1,0,3:T(2,128)(2,1)}), bf16[1,1,2,256,256]{4,2,1,0,3:T(2,128)(2,1)S(1)}, u32[]{:S(2)}, u32[]{:S(2)}) %all-to-all-start.1) | async-done | bytes 262176 | tf_op jit(solution)/shard_map/all_to_all | solution.py:156
  68.9 6.4 %all-to-all-start.4 = ((bf16[1,1,2,256,256]{4,2,1,0,3:T(2,128)(2,1)}), bf16[1,1,2,256,256]{4,2,1,0,3:T(2,128)(2,1)S(1)}, u32[]{:S(2)}, u32[]{:S(2)}) async-start(bf16[1,1,2,256,256]{4,2,1,0,3:T(2,128)(2,1)} %copy.44), calls=%async_computation.4 | async-start | bytes 524288 | tf_op jit(solution)/shard_map/all_to_all | solution.py:158
  81.0 13.9 %all-to-all-done.4 = bf16[1,1,2,256,256]{4,2,1,0,3:T(2,128)(2,1)S(1)} async-done(((bf16[1,1,2,256,256]{4,2,1,0,3:T(2,128)(2,1)}), bf16[1,1,2,256,256]{4,2,1,0,3:T(2,128)(2,1)S(1)}, u32[]{:S(2)}, u32[]{:S(2)}) %all-to-all-start.4) | async-done | bytes 262176 | tf_op jit(solution)/shard_map/all_to_all | solution.py:158
  95.0 6.7 %all-to-all-start.3 = ((bf16[1,1,2,256,256]{4,2,1,0,3:T(2,128)(2,1)}), bf16[1,1,2,256,256]{4,2,1,0,3:T(2,128)(2,1)S(1)}, u32[]{:S(2)}, u32[]{:S(2)}) async-start(bf16[1,1,2,256,256]{4,2,1,0,3:T(2,128)(2,1)} %copy.42), calls=%async_computation.3 | async-start | bytes 524288 | tf_op jit(solution)/shard_map/all_to_all | solution.py:157
  108.9 12.0 %all-to-all-done.3 = bf16[1,1,2,256,256]{4,2,1,0,3:T(2,128)(2,1)S(1)} async-done(((bf16[1,1,2,256,256]{4,2,1,0,3:T(2,128)(2,1)}), bf16[1,1,2,256,256]{4,2,1,0,3:T(2,128)(2,1)S(1)}, u32[]{:S(2)}, u32[]{:S(2)}) %all-to-all-start.3) | async-done | bytes 262176 | tf_op jit(solution)/shard_map/all_to_all | solution.py:157
  147.1 2.0 convolution_add_fusion.19
  157.4 6.6 %all-to-all-start.2 = ((bf16[64,1,2,4,256]{4,3,2,1,0:T(4,128)(2,1)}), bf16[64,1,2,4,256]{4,3,2,1,0:T(4,128)(2,1)S(1)}, u32[]{:S(2)}, u32[]{:S(2)}) async-start(bf16[64,1,2,4,256]{4,3,2,1,0:T(4,128)(2,1)} %fusion.38), calls=%async_computation.2 | async-start | bytes 524288 | tf_op jit(solution)/shard_map/all_to_all | solution.py:146
  167.6 15.7 %all-to-all-done.2 = bf16[64,1,2,4,256]{4,3,2,1,0:T(4,128)(2,1)S(1)} async-done(((bf16[64,1,2,4,256]{4,3,2,1,0:T(4,128)(2,1)}), bf16[64,1,2,4,256]{4,3,2,1,0:T(4,128)(2,1)S(1)}, u32[]{:S(2)}, u32[]{:S(2)}) %all-to-all-start.2) | async-done | bytes 262176 | tf_op jit(solution)/shard_map/all_to_all | solution.py:146
  183.3 6.5 %all-to-all-start.5 = ((bf16[64,1,2,4,256]{4,3,2,1,0:T(4,128)(2,1)}), bf16[64,1,2,4,256]{4,3,2,1,0:T(4,128)(2,1)S(1)}, u32[]{:S(2)}, u32[]{:S(2)}) async-start(bf16[64,1,2,4,256]{4,3,2,1,0:T(4,128)(2,1)} %fusion.40), calls=%async_computation.5 | async-start | bytes 524288 | tf_op jit(solution)/shard_map/all_to_all | solution.py:147
  192.9 61.4 %while.13 = (s32[]{:T(128)}, f32[1,2,256,256]{3,2,1,0:T(8,128)S(1)}, s32[]{:T(128)}, f32[1,1,2,256,256]{4,3,2,1,0:T(8,128)S(1)}, f32[1,1,2,256,256]{4,3,2,1,0:T(8,128)S(1)}, /*index=5*/s32[]{:T(128)}, s32[]{:T(128)}) while((s32[]{:T(128)}, f32[1,2,256,256]{3,2,1,0:T(8,128)S(1)}, s32[]{:T(128)}, ...), condition=%wide.region_3.4_spmd.clone, body=%wide.region_0.3_spmd.clone.sunk | while | flops 1611792384 | bytes 12058808 | solution.py:185
  193.1 1.9 collective-permute-start
  195.0 5.8 %collective-permute-done = bf16[1,2,256,256]{3,2,1,0:T(8,128)(2,1)S(1)} collective-permute-done((bf16[1,2,256,256]{3,2,1,0:T(8,128)(2,1)S(1)}, bf16[1,2,256,256]{3,2,1,0:T(8,128)(2,1)S(1)}, u32[]{:S(2)}, u32[]{:S(2)}) %collective-permute-start) | collective-permute-done | bytes 262176 | tf_op jit(solution)/shard_map/while/body/eval_jaxpr/ppermute | solution.py:12
  203.0 5.8 %collective-permute-done = bf16[1,2,256,256]{3,2,1,0:T(8,128)(2,1)S(1)} collective-permute-done((bf16[1,2,256,256]{3,2,1,0:T(8,128)(2,1)S(1)}, bf16[1,2,256,256]{3,2,1,0:T(8,128)(2,1)S(1)}, u32[]{:S(2)}, u32[]{:S(2)}) %collective-permute-start) | collective-permute-done | bytes 262176 | tf_op jit(solution)/shard_map/while/body/eval_jaxpr/ppermute | solution.py:12
  210.9 5.8 %collective-permute-done = bf16[1,2,256,256]{3,2,1,0:T(8,128)(2,1)S(1)} collective-permute-done((bf16[1,2,256,256]{3,2,1,0:T(8,128)(2,1)S(1)}, bf16[1,2,256,256]{3,2,1,0:T(8,128)(2,1)S(1)}, u32[]{:S(2)}, u32[]{:S(2)}) %collective-permute-start) | collective-permute-done | bytes 262176 | tf_op jit(solution)/shard_map/while/body/eval_jaxpr/ppermute | solution.py:12
  218.9 5.8 %collective-permute-done = bf16[1,2,256,256]{3,2,1,0:T(8,128)(2,1)S(1)} collective-permute-done((bf16[1,2,256,256]{3,2,1,0:T(8,128)(2,1)S(1)}, bf16[1,2,256,256]{3,2,1,0:T(8,128)(2,1)S(1)}, u32[]{:S(2)}, u32[]{:S(2)}) %collective-permute-start) | collective-permute-done | bytes 262176 | tf_op jit(solution)/shard_map/while/body/eval_jaxpr/ppermute | solution.py:12
  224.9 1.9 collective-permute-start
  226.8 5.8 %collective-permute-done = bf16[1,2,256,256]{3,2,1,0:T(8,128)(2,1)S(1)} collective-permute-done((bf16[1,2,256,256]{3,2,1,0:T(8,128)(2,1)S(1)}, bf16[1,2,256,256]{3,2,1,0:T(8,128)(2,1)S(1)}, u32[]{:S(2)}, u32[]{:S(2)}) %collective-permute-start) | collective-permute-done | bytes 262176 | tf_op jit(solution)/shard_map/while/body/eval_jaxpr/ppermute | solution.py:12
  234.8 8.1 %collective-permute-done = bf16[1,2,256,256]{3,2,1,0:T(8,128)(2,1)S(1)} collective-permute-done((bf16[1,2,256,256]{3,2,1,0:T(8,128)(2,1)S(1)}, bf16[1,2,256,256]{3,2,1,0:T(8,128)(2,1)S(1)}, u32[]{:S(2)}, u32[]{:S(2)}) %collective-permute-start) | collective-permute-done | bytes 262176 | tf_op jit(solution)/shard_map/while/body/eval_jaxpr/ppermute | solution.py:12
  243.2 3.3 %conditional.3 = (bf16[1,2,256,256]{3,2,1,0:T(8,128)(2,1)S(1)}) conditional(s32[]{:T(128)} %convert_element_type.868, () %tuple.60, (f32[1,1,2,256,256]{4,3,2,1,0:T(8,128)S(1)}, f32[1,1,2,256,256]{4,3,2,1,0:T(8,128)S(1)}, f32[1,2,256,256]{3,2,1,0:T(8,128)S(1)}) %tuple.61), branch_computations={%region_1.1_spmd, %region_2.2_spmd} | conditional | flops 1611268096 | bytes 8650760 | solution.py:181
  248.4 5.8 %collective-permute-done = bf16[1,2,256,256]{3,2,1,0:T(8,128)(2,1)S(1)} collective-permute-done((bf16[1,2,256,256]{3,2,1,0:T(8,128)(2,1)S(1)}, bf16[1,2,256,256]{3,2,1,0:T(8,128)(2,1)S(1)}, u32[]{:S(2)}, u32[]{:S(2)}) %collective-permute-start) | collective-permute-done | bytes 262176 | tf_op jit(solution)/shard_map/while/body/eval_jaxpr/ppermute | solution.py:12
  (188 shorter events, 76.8 us)
Async XLA Ops:
  2.6 18.7 %copy-start.19 = (bf16[1,1,2,256,256]{4,3,2,1,0:T(8,128)(2,1)S(1)}, bf16[1,1,2,256,256]{4,3,2,1,0:T(8,128)(2,1)}, u32[]{:S(2)}) copy-start(bf16[1,1,2,256,256]{4,3,2,1,0:T(8,128)(2,1)} %param.11) | copy-start | bytes 786436
  2.6 39.7 %all-to-all-start = ((bf16[1,1,2,256,256]{4,2,1,0,3:T(2,128)(2,1)}), bf16[1,1,2,256,256]{4,2,1,0,3:T(2,128)(2,1)S(1)}, u32[]{:S(2)}, u32[]{:S(2)}) async-start(bf16[1,1,2,256,256]{4,2,1,0,3:T(2,128)(2,1)} %copy.34), calls=%async_computation | async-start | bytes 524288 | tf_op jit(solution)/shard_map/all_to_all | solution.py:155
  22.2 26.5 %copy-start.20 = (bf16[1,1,2,256,256]{4,3,2,1,0:T(8,128)(2,1)S(1)}, bf16[1,1,2,256,256]{4,3,2,1,0:T(8,128)(2,1)}, u32[]{:S(2)}) copy-start(bf16[1,1,2,256,256]{4,3,2,1,0:T(8,128)(2,1)} %param.13) | copy-start | bytes 786436
  42.2 26.7 %all-to-all-start.1 = ((bf16[1,1,2,256,256]{4,2,1,0,3:T(2,128)(2,1)}), bf16[1,1,2,256,256]{4,2,1,0,3:T(2,128)(2,1)S(1)}, u32[]{:S(2)}, u32[]{:S(2)}) async-start(bf16[1,1,2,256,256]{4,2,1,0,3:T(2,128)(2,1)} %copy.36), calls=%async_computation.1 | async-start | bytes 524288 | tf_op jit(solution)/shard_map/all_to_all | solution.py:156
  52.1 82.9 %copy-start.2 = (bf16[64,1,2,1024]{3,0,2,1:T(8,128)(2,1)}, bf16[64,1,2,1024]{3,0,2,1:T(8,128)(2,1)S(1)}, u32[]{:S(2)}) copy-start(bf16[64,1,2,1024]{3,0,2,1:T(8,128)(2,1)S(1)} %reshape.780) | copy-start | bytes 786436
  68.9 26.0 %all-to-all-start.4 = ((bf16[1,1,2,256,256]{4,2,1,0,3:T(2,128)(2,1)}), bf16[1,1,2,256,256]{4,2,1,0,3:T(2,128)(2,1)S(1)}, u32[]{:S(2)}, u32[]{:S(2)}) async-start(bf16[1,1,2,256,256]{4,2,1,0,3:T(2,128)(2,1)} %copy.44), calls=%async_computation.4 | async-start | bytes 524288 | tf_op jit(solution)/shard_map/all_to_all | solution.py:158
  95.0 25.9 %all-to-all-start.3 = ((bf16[1,1,2,256,256]{4,2,1,0,3:T(2,128)(2,1)}), bf16[1,1,2,256,256]{4,2,1,0,3:T(2,128)(2,1)S(1)}, u32[]{:S(2)}, u32[]{:S(2)}) async-start(bf16[1,1,2,256,256]{4,2,1,0,3:T(2,128)(2,1)} %copy.42), calls=%async_computation.3 | async-start | bytes 524288 | tf_op jit(solution)/shard_map/all_to_all | solution.py:157
  124.5 1.0 copy-start.8
  125.6 1.0 copy-start.9
  126.6 1.0 copy-start.10
  127.7 1.0 copy-start.11
  130.4 1.0 copy-start.5
  132.5 1.0 copy-start.7
  147.1 2.0 copy-start.18
  153.4 1.3 copy-start.16
  157.4 25.9 %all-to-all-start.2 = ((bf16[64,1,2,4,256]{4,3,2,1,0:T(4,128)(2,1)}), bf16[64,1,2,4,256]{4,3,2,1,0:T(4,128)(2,1)S(1)}, u32[]{:S(2)}, u32[]{:S(2)}) async-start(bf16[64,1,2,4,256]{4,3,2,1,0:T(4,128)(2,1)} %fusion.38), calls=%async_computation.2 | async-start | bytes 524288 | tf_op jit(solution)/shard_map/all_to_all | solution.py:146
  183.3 71.6 %all-to-all-start.5 = ((bf16[64,1,2,4,256]{4,3,2,1,0:T(4,128)(2,1)}), bf16[64,1,2,4,256]{4,3,2,1,0:T(4,128)(2,1)S(1)}, u32[]{:S(2)}, u32[]{:S(2)}) async-start(bf16[64,1,2,4,256]{4,3,2,1,0:T(4,128)(2,1)} %fusion.40), calls=%async_computation.5 | async-start | bytes 524288 | tf_op jit(solution)/shard_map/all_to_all | solution.py:147
  193.1 7.7 %collective-permute-start = (bf16[1,2,256,256]{3,2,1,0:T(8,128)(2,1)S(1)}, bf16[1,2,256,256]{3,2,1,0:T(8,128)(2,1)S(1)}, u32[]{:S(2)}, u32[]{:S(2)}) collective-permute-start(bf16[1,2,256,256]{3,2,1,0:T(8,128)(2,1)S(1)} %get-tuple-element.250), channel_id=1, source_target_pairs={{0,64},{64,128},{128,192},{192,256},{256,320},{320,384},{384,448},... | collective-permute-start | bytes 786440 | tf_op jit(solution)/shard_map/while/body/eval_jaxpr/ppermute | solution.py:12
  201.0 7.7 %collective-permute-start = (bf16[1,2,256,256]{3,2,1,0:T(8,128)(2,1)S(1)}, bf16[1,2,256,256]{3,2,1,0:T(8,128)(2,1)S(1)}, u32[]{:S(2)}, u32[]{:S(2)}) collective-permute-start(bf16[1,2,256,256]{3,2,1,0:T(8,128)(2,1)S(1)} %get-tuple-element.250), channel_id=1, source_target_pairs={{0,64},{64,128},{128,192},{192,256},{256,320},{320,384},{384,448},... | collective-permute-start | bytes 786440 | tf_op jit(solution)/shard_map/while/body/eval_jaxpr/ppermute | solution.py:12
  209.0 7.7 %collective-permute-start = (bf16[1,2,256,256]{3,2,1,0:T(8,128)(2,1)S(1)}, bf16[1,2,256,256]{3,2,1,0:T(8,128)(2,1)S(1)}, u32[]{:S(2)}, u32[]{:S(2)}) collective-permute-start(bf16[1,2,256,256]{3,2,1,0:T(8,128)(2,1)S(1)} %get-tuple-element.250), channel_id=1, source_target_pairs={{0,64},{64,128},{128,192},{192,256},{256,320},{320,384},{384,448},... | collective-permute-start | bytes 786440 | tf_op jit(solution)/shard_map/while/body/eval_jaxpr/ppermute | solution.py:12
  216.9 7.7 %collective-permute-start = (bf16[1,2,256,256]{3,2,1,0:T(8,128)(2,1)S(1)}, bf16[1,2,256,256]{3,2,1,0:T(8,128)(2,1)S(1)}, u32[]{:S(2)}, u32[]{:S(2)}) collective-permute-start(bf16[1,2,256,256]{3,2,1,0:T(8,128)(2,1)S(1)} %get-tuple-element.250), channel_id=1, source_target_pairs={{0,64},{64,128},{128,192},{192,256},{256,320},{320,384},{384,448},... | collective-permute-start | bytes 786440 | tf_op jit(solution)/shard_map/while/body/eval_jaxpr/ppermute | solution.py:12
  224.9 7.7 %collective-permute-start = (bf16[1,2,256,256]{3,2,1,0:T(8,128)(2,1)S(1)}, bf16[1,2,256,256]{3,2,1,0:T(8,128)(2,1)S(1)}, u32[]{:S(2)}, u32[]{:S(2)}) collective-permute-start(bf16[1,2,256,256]{3,2,1,0:T(8,128)(2,1)S(1)} %get-tuple-element.250), channel_id=1, source_target_pairs={{0,64},{64,128},{128,192},{192,256},{256,320},{320,384},{384,448},... | collective-permute-start | bytes 786440 | tf_op jit(solution)/shard_map/while/body/eval_jaxpr/ppermute | solution.py:12
  232.9 10.1 %collective-permute-start = (bf16[1,2,256,256]{3,2,1,0:T(8,128)(2,1)S(1)}, bf16[1,2,256,256]{3,2,1,0:T(8,128)(2,1)S(1)}, u32[]{:S(2)}, u32[]{:S(2)}) collective-permute-start(bf16[1,2,256,256]{3,2,1,0:T(8,128)(2,1)S(1)} %get-tuple-element.250), channel_id=1, source_target_pairs={{0,64},{64,128},{128,192},{192,256},{256,320},{320,384},{384,448},... | collective-permute-start | bytes 786440 | tf_op jit(solution)/shard_map/while/body/eval_jaxpr/ppermute | solution.py:12
  246.5 7.7 %collective-permute-start = (bf16[1,2,256,256]{3,2,1,0:T(8,128)(2,1)S(1)}, bf16[1,2,256,256]{3,2,1,0:T(8,128)(2,1)S(1)}, u32[]{:S(2)}, u32[]{:S(2)}) collective-permute-start(bf16[1,2,256,256]{3,2,1,0:T(8,128)(2,1)S(1)} %get-tuple-element.250), channel_id=1, source_target_pairs={{0,64},{64,128},{128,192},{192,256},{256,320},{320,384},{384,448},... | collective-permute-start | bytes 786440 | tf_op jit(solution)/shard_map/while/body/eval_jaxpr/ppermute | solution.py:12
  (11 other events, 10.8 us)
where the time goes:
time: 260 us; the launch traced here: 258 us
  waiting for transfers between devices  121 us (47%)
  starting transfers between devices  64.7 us (25%)
  matrix products  43.7 us (17%)
  local copies, waits for them, and re-layouts  23.2 us (9%)
  other arithmetic  3.92 us (2%)
    ppermute x7, waiting for transfers between devices, from_behind(): return lax.ppermute(array, axis, pairs)  42.6 us
    all_to_all x1, waiting for transfers between devices, body(): lax.all_to_all(green_lesser, 'energy', split_axis=3, concat_axis=0, tiled...  20 us
    all_to_all x1, starting transfers between devices, body(): lax.all_to_all(green_lesser, 'energy', split_axis=3, concat_axis=0, tiled...  18.7 us
    all_to_all x1, waiting for transfers between devices, body(): lax.all_to_all(screened_lesser, 'energy', split_axis=3, concat_axis=0, ti...  16.8 us
    all_to_all x1, waiting for transfers between devices, convolve(): lax.all_to_all(lesser_sigma, 'energy', split_axis=0, concat_axis=3, tiled...  15.7 us
    unnamed x50, local copies, waits for them, and re-layouts  14.2 us
    all_to_all x1, waiting for transfers between devices, body(): lax.all_to_all(screened_retarded, 'energy', split_axis=3, concat_axis=0,...  13.9 us
    ppermute x7, starting transfers between devices, from_behind(): return lax.ppermute(array, axis, pairs)  13.4 us
  transfers between devices with their start and end apart: 13, of which 12 were waited for; matrix products, arithmetic and copies ran while one was open for 10% of the time, Pallas kernels for 0%

commit v1 on v0

v1 whole, which is shorter than its diff:
```python
import functools
import math

import jax
import jax.numpy as jnp
import ml_dtypes
import numpy as np
from jax import lax
from jax.experimental import pallas as pl
from jax.experimental.pallas import tpu as pltpu
from jax.sharding import PartitionSpec as P

MESH = pl.DeviceIdType.MESH
BF16 = jnp.bfloat16
F32 = jnp.float32
NE = 64
LENGTH = 96
LAG = 32


def split_table(table):
    upper = table.astype(ml_dtypes.bfloat16)
    lower = (table - upper.astype(np.float64)).astype(ml_dtypes.bfloat16)
    return np.stack([upper, lower])


def tables():
    step = 2.0 * math.pi / LENGTH
    k = np.arange(LENGTH)
    n = np.arange(NE)
    angle = (k[:, None] * n[None, :] % LENGTH) * step
    forward = np.block([[np.cos(angle), np.sin(angle)], [-np.sin(angle), np.cos(angle)]])
    angle = ((n[:, None] + LAG) * k[None, :] % LENGTH) * step
    back = np.block([[np.cos(angle), -np.sin(angle)], [np.sin(angle), np.cos(angle)]]) / LENGTH
    return split_table(forward), split_table(back)


def dot(first, second):
    return jnp.dot(first, second, preferred_element_type=F32)


def dot_t(first, second):
    return lax.dot_general(first, second, (((1,), (1,)), ((), ())), preferred_element_type=F32)


def product(a_re, a_im, b_re, b_im):
    return dot(a_re, b_re) - dot(a_im, b_im), dot(a_re, b_im) + dot(a_im, b_re)


def adjoint(a_re, a_im, b_re, b_im):
    return dot_t(a_re, b_re) + dot_t(a_im, b_im), dot_t(a_im, b_re) - dot_t(a_re, b_im)


def sandwich(p_ref, s_ref):
    p_re, p_im = p_ref[0], p_ref[1]
    i_re, i_im = product(p_re, p_im, s_ref[0], s_ref[1])
    return adjoint(i_re.astype(BF16), i_im.astype(BF16), p_re, p_im)


def pack(src, dst):
    @pl.loop(0, 16)
    def _(b):
        for cb in range(2):
            re = src[0, pl.ds(16 * b, 16), 128 * cb : 128 * cb + 128].astype(F32)
            im = src[1, pl.ds(16 * b, 16), 128 * cb : 128 * cb + 128].astype(F32)
            for h in range(2):
                both = jnp.concatenate([re[8 * h : 8 * h + 8], im[8 * h : 8 * h + 8]], axis=0)
                dst[4 * b + 2 * h + cb, :, :] = both.astype(BF16)


def unpack(src, dst):
    @pl.loop(0, 16)
    def _(b):
        for cb in range(2):
            low = src[4 * b + cb].astype(F32)
            high = src[4 * b + 2 + cb].astype(F32)
            for part in range(2):
                rows = slice(8 * part, 8 * part + 8)
                both = jnp.concatenate([low[rows], high[rows]], axis=0)
                dst[part, pl.ds(16 * b, 16), 128 * cb : 128 * cb + 128] = both.astype(BF16)


def stage(received, wide):
    @pl.loop(0, 16)
    def _(i):
        wide[pl.ds(64 * i, 64), :] = received[pl.ds(4 * i, 4)].reshape(64, 128).astype(F32)


def gather_columns(wide, q):
    columns = []
    for s in (2 * q, 2 * q + 1):
        re = wide[pl.ds(s, NE, 16), :]
        im = wide[pl.ds(8 + s, NE, 16), :]
        columns.append(jnp.concatenate([re, im], axis=0))
    return jnp.concatenate(columns, axis=1).astype(BF16)


def spectrum(wide, forward, q):
    columns = gather_columns(wide, q)
    both = dot(forward[0], columns) + dot(forward[1], columns)
    return both[:LENGTH], both[LENGTH:]


def times(a, b):
    return a[0] * b[0] - a[1] * b[1], a[0] * b[1] + a[1] * b[0]


def back_to_energy(hat, back, wide, q):
    both = jnp.concatenate(hat, axis=0)
    upper = both.astype(BF16)
    lower = (both - upper.astype(F32)).astype(BF16)
    values = dot(back[0], upper) + dot(back[1], upper) + dot(back[0], lower)
    for i, s in enumerate((2 * q, 2 * q + 1)):
        wide[pl.ds(s, NE, 16), :] = values[:NE, 128 * i : 128 * i + 128]
        wide[pl.ds(8 + s, NE, 16), :] = values[NE:, 128 * i : 128 * i + 128]


def narrow(wide, dst):
    @pl.loop(0, 16)
    def _(i):
        dst[pl.ds(4 * i, 4)] = wide[pl.ds(64 * i, 64), :].reshape(4, 16, 128).astype(BF16)


def kernel(
    gl, wl, gr, wr, lg, cp, fwd, bwd, out_l, out_r,
    s_gl, s_wl, s_gr, s_wr, r_gl, r_wl, r_gr, r_wr, o_l, o_r, q_l, q_r,
    wide_a, wide_b, f_gl, f_wl, f_gr,
    sig, prop, trans, src, half, in_p, in_s, in_e,
    e_send, e_recv, s_send, s_recv,
):
    me = lax.axis_index("energy")
    pos = lax.axis_index("space")
    y, core = pos // 2, pos % 2

    barrier = pltpu.get_barrier_semaphore()

    @pl.loop(1, NE)
    def _(s):
        pl.semaphore_signal(barrier, inc=1, device_id={"energy": lax.rem(me + s, NE)}, device_id_type=MESH)

    @pl.loop(1, 8)
    def _(s):
        pl.semaphore_signal(barrier, inc=1, device_id={"space": lax.rem(pos + s, 8)}, device_id_type=MESH)

    pack(gl, s_gl)
    pack(wl, s_wl)
    pack(gr, s_gr)
    pack(wr, s_wr)
    pl.semaphore_wait(barrier, NE - 1 + 7)

    def exchange(slot, *pairs):
        @pl.loop(1, NE)
        def _(s):
            peer = lax.rem(me + s, NE)
            for i, (source, target) in enumerate(pairs):
                pltpu.make_async_remote_copy(
                    src_ref=source.at[peer],
                    dst_ref=target.at[me],
                    send_sem=e_send.at[slot + i],
                    recv_sem=e_recv.at[slot + i],
                    device_id={"energy": peer},
                    device_id_type=MESH,
                ).start()

        for source, target in pairs:
            target[me] = source[me]

    def wait_recv(slot, buffer):
        pltpu.make_async_copy(buffer.at[pl.ds(0, NE - 1)], buffer.at[pl.ds(0, NE - 1)], e_recv.at[slot]).wait()

    def wait_send(slot, buffer):
        pltpu.make_async_copy(buffer.at[pl.ds(0, NE - 1)], buffer.at[pl.ds(0, NE - 1)], e_send.at[slot]).wait()

    def to_space(slot, source, target, where):
        return pltpu.make_async_remote_copy(
            src_ref=source,
            dst_ref=target,
            send_sem=s_send.at[slot],
            recv_sem=s_recv.at[slot],
            device_id={"space": where},
            device_id_type=MESH,
        )

    exchange(0, (s_gl, r_gl), (s_wl, r_wl))
    exchange(2, (s_gr, r_gr))

    p_re, p_im = product(lg[0], lg[1], cp[0], cp[1])
    prop[0] = p_re.astype(BF16)
    prop[1] = p_im.astype(BF16)
    p_over = to_space(0, prop, in_p, lax.rem(pos + 1, 8))

    @pl.when(core == 0)
    def _():
        p_over.start()
        p_over.wait_send()

    @pl.when(core == 1)
    def _():
        p_over.wait_recv()
        t_re, t_im = product(prop[0], prop[1], in_p[0], in_p[1])
        trans[0] = t_re.astype(BF16)
        trans[1] = t_im.astype(BF16)

    wait_recv(0, r_gl)
    wait_recv(1, r_wl)
    stage(r_gl, wide_a)
    stage(r_wl, wide_b)
    for q in range(4):
        f_gl[q, 0], f_gl[q, 1] = spectrum(wide_a, fwd, q)
        f_wl[q, 0], f_wl[q, 1] = spectrum(wide_b, fwd, q)
    for q in range(4):
        hat = times((f_gl[q, 0], f_gl[q, 1]), (f_wl[q, 0], f_wl[q, 1]))
        back_to_energy(hat, bwd, wide_a, q)
    narrow(wide_a, o_l)
    exchange(4, (o_l, q_l))
    exchange(3, (s_wr, r_wr))

    wait_recv(2, r_gr)
    stage(r_gr, wide_a)
    for q in range(4):
        f_gr[q, 0], f_gr[q, 1] = spectrum(wide_a, fwd, q)

    wait_recv(4, q_l)
    unpack(q_l, sig)
    h_re, h_im = product(lg[0], lg[1], sig[0], sig[1])
    half[0] = h_re.astype(BF16)
    half[1] = h_im.astype(BF16)
    src[0], src[1] = adjoint(half[0], half[1], lg[0], lg[1])
    s_over = to_space(1, half, in_s, lax.rem(pos + 1, 8))

    @pl.when(core == 0)
    def _():
        half[0] = src[0].astype(BF16)
        half[1] = src[1].astype(BF16)
        s_over.start()

    @pl.when(core == 1)
    def _():
        s_over.wait_recv()
        a_re, a_im = sandwich(prop, in_s)
        src[0] += a_re
        src[1] += a_im

    def finish_retarded():
        wait_recv(3, r_wr)
        stage(r_wr, wide_b)
        for q in range(4):
            w_r = spectrum(wide_b, fwd, q)
            w_l = (f_wl[q, 0], f_wl[q, 1])
            first = times((f_gr[q, 0], f_gr[q, 1]), (w_l[0] + w_r[0], w_l[1] + w_r[1]))
            second = times((f_gl[q, 0], f_gl[q, 1]), w_r)
            back_to_energy((first[0] + second[0], first[1] + second[1]), bwd, wide_a, q)
        narrow(wide_a, o_r)
        exchange(5, (o_r, q_r))

    finish_retarded()

    e_ahead = to_space(2, out_l, in_e, lax.rem(pos + 2, 8))
    e_beside = to_space(3, in_e, in_e, lax.rem(pos + 7, 8))

    @pl.when(core == 0)
    def _():
        s_over.wait_send()

        @pl.when(y == 0)
        def _():
            out_l[...] = src[...].astype(BF16)

        @pl.when(y > 0)
        def _():
            e_beside.wait_recv()
            a_re, a_im = sandwich(prop, in_e)
            out_l[0] = (src[0] + a_re).astype(BF16)
            out_l[1] = (src[1] + a_im).astype(BF16)

    @pl.when(core == 1)
    def _():
        @pl.when(y == 0)
        def _():
            out_l[...] = src[...].astype(BF16)

        @pl.when(y > 0)
        def _():
            e_ahead.wait_recv()
            e_beside.start()
            a_re, a_im = sandwich(trans, in_e)
            out_l[0] = (src[0] + a_re).astype(BF16)
            out_l[1] = (src[1] + a_im).astype(BF16)

        @pl.when(y < 3)
        def _():
            e_ahead.start()

        @pl.when(y > 0)
        def _():
            e_beside.wait_send()

        @pl.when(y < 3)
        def _():
            e_ahead.wait_send()

    wait_recv(5, q_r)
    unpack(q_r, out_r)
    for slot, buffer in enumerate((s_gl, s_wl, s_gr, s_wr, o_l, o_r)):
        wait_send(slot, buffer)


def body(green_lesser, screened_lesser, green_retarded, screened_retarded, left_green, coupling):
    blocks = [a[0, 0] for a in (green_lesser, screened_lesser, green_retarded, screened_retarded, left_green)]
    forward, back = tables()
    block = blocks[0].shape
    vmem = pl.BlockSpec(memory_space=pltpu.VMEM)
    chunks = pltpu.VMEM((NE, 16, 128), BF16)
    spectra = pltpu.VMEM((4, 2, LENGTH, 256), F32)
    whole = pltpu.VMEM(block, BF16)
    out_l, out_r = pl.pallas_call(
        kernel,
        out_shape=[jax.ShapeDtypeStruct(block, BF16)] * 2,
        in_specs=[vmem] * 8,
        out_specs=[vmem] * 2,
        scratch_shapes=[chunks] * 12
        + [pltpu.VMEM((NE * 16, 128), F32)] * 2
        + [spectra] * 3
        + [whole, whole, whole, pltpu.VMEM(block, F32), whole, whole, whole, whole]
        + [pltpu.SemaphoreType.DMA((6,)), pltpu.SemaphoreType.DMA((6,))]
        + [pltpu.SemaphoreType.DMA((4,)), pltpu.SemaphoreType.DMA((4,))],
        compiler_params=pltpu.CompilerParams(
            collective_id=0, has_side_effects=True, vmem_limit_bytes=48 * 2**20
        ),
    )(*blocks, coupling[0], jnp.asarray(forward), jnp.asarray(back))
    return out_l[None, None], out_r[None, None]


def solution(mesh):
    point = P("energy", "space", None, None, None)
    return jax.shard_map(
        body,
        mesh=mesh,
        in_specs=(point,) * 5 + (P("space", None, None, None),),
        out_specs=(point, point),
        check_vma=False,
    )
```

time: 260 us -> 103 us (0.40)
  waiting for transfers between devices: 121 us -> 0 us
  Pallas kernels: 0 us -> 93.5 us
  starting transfers between devices: 64.7 us -> 0 us
  matrix products: 43.7 us -> 0 us
  local copies, waits for them, and re-layouts: 23.2 us -> 8.89 us
  other arithmetic: 3.92 us -> 0 us
    pallas_call x0 -> x1, Pallas kernels: none -> 93.5 us  [body(): pl.pallas_call(kernel, out_shape=[jax.ShapeDtypeStruct(block, BF16)] * 2,...]
    all_to_all x6 -> x0, waiting for transfers between devices: 78.4 us -> none  [the longest x1 20 us: body(): lax.all_to_all(green_lesser, 'energy', split_axis=3, concat_axis=0, tiled...]
    all_to_all x6 -> x0, starting transfers between devices: 51.3 us -> none  [the longest x1 18.7 us: body(): lax.all_to_all(green_lesser, 'energy', split_axis=3, concat_axis=0, tiled...]
    dot_general x84 -> x0, matrix products: 43.7 us -> none  [the longest x16 13.3 us: table_product(): jnp.einsum('jz,zgx->jgx', trig_table_pair[0], slab_values, preferred_elem...]
    ppermute x7 -> x0, waiting for transfers between devices: 42.6 us -> none  [from_behind(): return lax.ppermute(array, axis, pairs)]
    ppermute x7 -> x0, starting transfers between devices: 13.4 us -> none  [from_behind(): return lax.ppermute(array, axis, pairs)]
    unnamed x50 -> x18, local copies, waits for them, and re-layouts: 14.2 us -> 8.89 us
    another operation x10 -> x0, local copies, waits for them, and re-layouts: 3.91 us -> none  [the longest x4 3.78 us: to_energy(): stacked = jnp.stack([real_part, imag_part], axis=2) * (1.0 / length)]
  transfers between devices with their start and end apart: 13 -> 0, of which waited for: 12 -> 0; matrix products, arithmetic and copies ran while one was open for 10% -> 0% of each run, Pallas kernels for 0% -> 0%
where the time goes in v1:
time: 103 us
  Pallas kernels  93.5 us (91%)
  local copies, waits for them, and re-layouts  8.89 us (9%)
    pallas_call x1, Pallas kernels, body(): pl.pallas_call(kernel, out_shape=[jax.ShapeDtypeStruct(block, BF16)] * 2,...  93.5 us
    unnamed x18, local copies, waits for them, and re-layouts  8.89 us

profile of v1, /device:TPU:24, one launch (start us, length us, event | category | flops | bytes accessed | tf_op | source)
XLA Modules:
  0.0 103.1 jit_solution(16368414245874147691)
XLA Ops:
  0.6 0.0 copy-start
  0.6 0.9 copy-done
  1.6 0.0 copy-start.1
  1.6 0.9 copy-done.1
  2.5 0.0 copy-start.2
  2.5 0.9 copy-done.2
  3.5 0.0 copy-start.3
  3.5 0.9 copy-done.3
  4.4 0.0 copy-start.4
  4.4 0.9 copy-done.4
  5.4 0.0 copy-start.5
  5.4 0.9 copy-done.5
  6.3 0.0 copy-start.6
  6.3 0.9 copy-done.6
  7.2 0.0 copy-start.7
  7.2 0.9 copy-done.7
  8.1 93.5 %shard_map.95 = (bf16[2,256,256]{2,1,0:T(8,128)(2,1)S(1)}, bf16[2,256,256]{2,1,0:T(8,128)(2,1)S(1)}) custom-call(bf16[2,256,256]{2,1,0:T(8,128)(2,1)S(1)} %bitcast.8, bf16[2,256,256]{2,1,0:T(8,128)(2,1)S(1)} %bitcast.9, bf16[2,256,256]{2,1,0:T(8,128)(2,1)S(1)} %bitcast.10, bf16[2,256,256]{2,1,0:T(8,128)(2,1)S(1)} %bitcast.11, ...), custom_call_target="tpu_custom_call" | custom-call | tf_op jit(solution)/shard_map/pallas_call | solution.py:316
  101.6 0.7 copy.12
  102.4 0.7 copy.13
Async XLA Ops:
  0.6 1.0 copy-start
  1.6 0.9 copy-start.1
  2.5 0.9 copy-start.2
  3.5 0.9 copy-start.3
  4.4 0.9 copy-start.4
  5.4 0.9 copy-start.5
  6.3 0.9 copy-start.6
  7.2 0.9 copy-start.7

commit v2 on v1

--- a/solution.py
+++ b/solution.py
@@ -122,16 +122,35 @@
 
 
 def kernel(
-    gl, wl, gr, wr, lg, cp, fwd, bwd, out_l, out_r,
+    hbm_gl, hbm_wl, hbm_gr, hbm_wr, hbm_lg, hbm_cp, hbm_fwd, hbm_bwd, out_l, out_r,
+    gl, wl, gr, wr, lg, cp, fwd, bwd,
     s_gl, s_wl, s_gr, s_wr, r_gl, r_wl, r_gr, r_wr, o_l, o_r, q_l, q_r,
     wide_a, wide_b, f_gl, f_wl, f_gr,
     sig, prop, trans, src, half, in_p, in_s, in_e,
-    e_send, e_recv, s_send, s_recv,
+    e_send, e_recv, s_send, s_recv, l_sem,
 ):
     me = lax.axis_index("energy")
     pos = lax.axis_index("space")
     y, core = pos // 2, pos % 2
 
+    loads = [
+        pltpu.make_async_copy(source, target, l_sem.at[i])
+        for i, (source, target) in enumerate(
+            (
+                (hbm_gl, gl),
+                (hbm_wl, wl),
+                (hbm_gr, gr),
+                (hbm_wr, wr),
+                (hbm_lg, lg),
+                (hbm_cp, cp),
+                (hbm_fwd, fwd),
+                (hbm_bwd, bwd),
+            )
+        )
+    ]
+    for load in loads:
+        load.start()
+
     barrier = pltpu.get_barrier_semaphore()
 
     @pl.loop(1, NE)
@@ -142,10 +161,11 @@
     def _(s):
         pl.semaphore_signal(barrier, inc=1, device_id={"space": lax.rem(pos + s, 8)}, device_id_type=MESH)
 
-    pack(gl, s_gl)
-    pack(wl, s_wl)
-    pack(gr, s_gr)
-    pack(wr, s_wr)
+    for load, source, target in zip(loads, (gl, wl, gr, wr), (s_gl, s_wl, s_gr, s_wr)):
+        load.wait()
+        pack(source, target)
+    for load in loads[4:]:
+        load.wait()
     pl.semaphore_wait(barrier, NE - 1 + 7)
 
     def exchange(slot, *pairs):
@@ -316,16 +336,18 @@
     out_l, out_r = pl.pallas_call(
         kernel,
         out_shape=[jax.ShapeDtypeStruct(block, BF16)] * 2,
-        in_specs=[vmem] * 8,
+        in_specs=[pl.BlockSpec(memory_space=pltpu.HBM)] * 8,
         out_specs=[vmem] * 2,
-        scratch_shapes=[chunks] * 12
+        scratch_shapes=[whole] * 6
+        + [pltpu.VMEM(forward.shape, BF16), pltpu.VMEM(back.shape, BF16)]
+        + [chunks] * 12
         + [pltpu.VMEM((NE * 16, 128), F32)] * 2
         + [spectra] * 3
         + [whole, whole, whole, pltpu.VMEM(block, F32), whole, whole, whole, whole]
         + [pltpu.SemaphoreType.DMA((6,)), pltpu.SemaphoreType.DMA((6,))]
-        + [pltpu.SemaphoreType.DMA((4,)), pltpu.SemaphoreType.DMA((4,))],
+        + [pltpu.SemaphoreType.DMA((4,)), pltpu.SemaphoreType.DMA((4,)), pltpu.SemaphoreType.DMA((8,))],
         compiler_params=pltpu.CompilerParams(
-            collective_id=0, has_side_effects=True, vmem_limit_bytes=48 * 2**20
+            collective_id=0, has_side_effects=True, vmem_limit_bytes=63 * 2**20
         ),
     )(*blocks, coupling[0], jnp.asarray(forward), jnp.asarray(back))
     return out_l[None, None], out_r[None, None]

time: 103 us -> 97.6 us (0.948)
  local copies, waits for them, and re-layouts: 8.89 us -> 2.42 us
    unnamed x18 -> x4, local copies, waits for them, and re-layouts: 8.89 us -> 2.42 us
where the time goes in v2:
time: 97.6 us; the launch traced here: 97.4 us
  Pallas kernels  94.3 us (97%)
  local copies, waits for them, and re-layouts  2.42 us (2%)
    pallas_call x1, Pallas kernels, body(): pl.pallas_call(kernel, out_shape=[jax.ShapeDtypeStruct(block, BF16)] * 2,...  94.3 us
    unnamed x4, local copies, waits for them, and re-layouts  2.42 us

profile of v2, /device:TPU:24, one launch (start us, length us, event | category | flops | bytes accessed | tf_op | source)
XLA Modules:
  0.0 97.4 jit_solution(1320866673658561960)
XLA Ops:
  0.6 94.3 %shard_map.95 = (bf16[2,256,256]{2,1,0:T(8,128)(2,1)}, bf16[2,256,256]{2,1,0:T(8,128)(2,1)}) custom-call(bf16[2,256,256]{2,1,0:T(8,128)(2,1)} %bitcast.8, bf16[2,256,256]{2,1,0:T(8,128)(2,1)} %bitcast.9, bf16[2,256,256]{2,1,0:T(8,128)(2,1)} %bitcast.10, bf16[2,256,256]{2,1,0:T(8,128)(2,1)} %bitcast.11, bf16[2,256,256]{2,1,0:T(8,128)(2,1)} %bitcast.12, ...), custom_call_target="tpu_custom_call" | custom-call | tf_op jit(solution)/shard_map/pallas_call | solution.py:336
  95.0 0.0 copy-start
  95.0 1.7 %copy.12 = bf16[1,1,2,256,256]{4,3,2,1,0:T(8,128)(2,1)} copy(bf16[1,1,2,256,256]{4,3,2,1,0:T(8,128)(2,1)} %bitcast.15) | data formatting | bytes 524288
  96.7 0.0 copy-done
  96.7 0.7 copy.13
Async XLA Ops:
  95.0 1.7 %copy-start = (bf16[2,256,256]{2,1,0:T(8,128)(2,1)S(1)}, bf16[2,256,256]{2,1,0:T(8,128)(2,1)}, u32[]{:S(2)}) copy-start(bf16[2,256,256]{2,1,0:T(8,128)(2,1)} %get-tuple-element.5) | copy-start | bytes 786436

commit v3 on v2

--- a/solution.py
+++ b/solution.py
@@ -273,18 +273,23 @@
         narrow(wide_a, o_r)
         exchange(5, (o_r, q_r))
 
-    finish_retarded()
-
     e_ahead = to_space(2, out_l, in_e, lax.rem(pos + 2, 8))
     e_beside = to_space(3, in_e, in_e, lax.rem(pos + 7, 8))
 
+    @pl.when(y == 0)
+    def _():
+        out_l[...] = src[...].astype(BF16)
+
+        @pl.when(core == 1)
+        def _():
+            e_ahead.start()
+
+    finish_retarded()
+
+
     @pl.when(core == 0)
     def _():
         s_over.wait_send()
-
-        @pl.when(y == 0)
-        def _():
-            out_l[...] = src[...].astype(BF16)
 
         @pl.when(y > 0)
         def _():
@@ -295,10 +300,6 @@
 
     @pl.when(core == 1)
     def _():
-        @pl.when(y == 0)
-        def _():
-            out_l[...] = src[...].astype(BF16)
-
         @pl.when(y > 0)
         def _():
             e_ahead.wait_recv()
@@ -307,7 +308,7 @@
             out_l[0] = (src[0] + a_re).astype(BF16)
             out_l[1] = (src[1] + a_im).astype(BF16)
 
-        @pl.when(y < 3)
+        @pl.when(jnp.logical_and(y > 0, y < 3))
         def _():
             e_ahead.start()
 

time: 97.6 us -> 96.4 us (0.988)
  Pallas kernels: 94.3 us -> 93.2 us
    pallas_call x1, Pallas kernels: 94.3 us -> 93.2 us  [body(): pl.pallas_call(kernel, out_shape=[jax.ShapeDtypeStruct(block, BF16)] * 2,...]
where the time goes in v3:
time: 96.4 us; the launch traced here: 96.2 us
  Pallas kernels  93.2 us (97%)
  local copies, waits for them, and re-layouts  2.42 us (3%)
    pallas_call x1, Pallas kernels, body(): pl.pallas_call(kernel, out_shape=[jax.ShapeDtypeStruct(block, BF16)] * 2,...  93.2 us
    unnamed x4, local copies, waits for them, and re-layouts  2.42 us

profile of v3, /device:TPU:24, one launch (start us, length us, event | category | flops | bytes accessed | tf_op | source)
XLA Modules:
  0.0 96.2 jit_solution(5330042165898029108)
XLA Ops:
  0.6 93.2 %shard_map.95 = (bf16[2,256,256]{2,1,0:T(8,128)(2,1)}, bf16[2,256,256]{2,1,0:T(8,128)(2,1)}) custom-call(bf16[2,256,256]{2,1,0:T(8,128)(2,1)} %bitcast.8, bf16[2,256,256]{2,1,0:T(8,128)(2,1)} %bitcast.9, bf16[2,256,256]{2,1,0:T(8,128)(2,1)} %bitcast.10, bf16[2,256,256]{2,1,0:T(8,128)(2,1)} %bitcast.11, bf16[2,256,256]{2,1,0:T(8,128)(2,1)} %bitcast.12, ...), custom_call_target="tpu_custom_call" | custom-call | tf_op jit(solution)/shard_map/pallas_call | solution.py:337
  93.8 0.0 copy-start
  93.8 1.7 %copy.12 = bf16[1,1,2,256,256]{4,3,2,1,0:T(8,128)(2,1)} copy(bf16[1,1,2,256,256]{4,3,2,1,0:T(8,128)(2,1)} %bitcast.15) | data formatting | bytes 524288
  95.5 0.0 copy-done
  95.5 0.7 copy.13
Async XLA Ops:
  93.8 1.7 %copy-start = (bf16[2,256,256]{2,1,0:T(8,128)(2,1)S(1)}, bf16[2,256,256]{2,1,0:T(8,128)(2,1)}, u32[]{:S(2)}) copy-start(bf16[2,256,256]{2,1,0:T(8,128)(2,1)} %get-tuple-element.5) | copy-start | bytes 786436
